TPU v7x, 256 devices: a whole 4x4x8 slice. The times are simulated.
256 devices in a mesh: team: 4 (over x), row: 8 (over z), col: 8 (over y, core).
Axes of the slice: x: 4, y: 4, z: 8, core: 2. Of those that a mesh axis runs over, the one named last changes fastest.
Arguments:
- child_inverse: bfloat16 [4, 8192, 8192], P('team', 'row', 'col'), may hold values from -0.125 to 0.125
- child_lower: bfloat16 [4, 8192, 8192], P('team', 'row', 'col'), may hold values from -0.0625 to 0.0625
- child_rhs: bfloat16 [4, 8192, 256], P('team', 'col'), may hold values from -6 to 6
- child_diag: float32 [4, 8192], P('team', 'row'), may hold values from -4 to 4, as said below
- child_off: float32 [4, 8192], P('team', 'row'), may hold values from -4 to 4
- child_pattern: int32 [4, 8192], P('team', 'row'), may hold values from 0 to 2, as said below
- child_pivots: int32 [4], P('team'), may hold values from 4096 to 8192, as said below
- child_map: int32 [4, 8192], P('team', 'col'), may hold values from 0 to 16383, as said below
- root_inverse: bfloat16 [16384, 16384], P('row', ('team', 'col')), may hold values from -0.09375 to 0.09375
- root_rhs: bfloat16 [16384, 256], P(('team', 'col')), may hold values from -6 to 6
- root_diag: float32 [16384], P('row'), may hold values from -4 to 4, as said below
- root_off: float32 [16384], P('row'), may hold values from -4 to 4
- root_pattern: int32 [16384], P('row'), may hold values from 0 to 2, as said below
Outputs:
- child_solution: float32 [4, 8192, 256], P('team', 'col')
- root_solution: float32 [16384, 256], P(('team', 'col'))
Inputs may be any that keep to these rules, and one draw needn't show every extreme that they name: `child_pivots`: one child has exactly 8192 live pivot rows. `child_pattern`: rows come in aligned pairs: (1, 2) marks a 2x2 pivot block, (0, 0) two 1x1 blocks. `root_pattern`: rows come in aligned pairs: (1, 2) marks a 2x2 pivot block, (0, 0) two 1x1 blocks. `child_diag`: magnitudes lie between 1 and 4, signs vary; the two diagonal entries of a 2x2 pivot block have opposite signs. `root_diag`: magnitudes lie between 1 and 4, signs vary; the two diagonal entries of a 2x2 pivot block have opposite signs. `child_map`: within one child the 8192 entries are distinct. With parent rows taken in aligned blocks of 512, every aligned block of 1024 entries of a child has at most 64 entries in any one parent block, and exactly 64 in some parent block.
All inputs are finite; a program needn't handle non-finite values.
Results may differ from a plain program's by a relative error of at most 0.013.
Values may be sent and summed in bfloat16 or wider, within the bound.
A program may use at most 64 MiB of HBM per device.

v0:
```python
import jax
import jax.numpy as jnp
from jax import lax
from jax.sharding import PartitionSpec as P


def pivot_solve(values, diagonal, offdiag, pattern):
    first_rows = values[0::2]
    second_rows = values[1::2]
    lead_diag = diagonal[0::2][:, None]
    next_diag = diagonal[1::2][:, None]
    coupling = jnp.where(pattern[0::2] == 1, offdiag[0::2], jnp.zeros_like(offdiag[0::2]))[:, None]
    determinant = lead_diag * next_diag - coupling * coupling
    solved_first = (next_diag * first_rows - coupling * second_rows) / determinant
    solved_second = (lead_diag * second_rows - coupling * first_rows) / determinant
    return jnp.stack([solved_first, solved_second], axis=1).reshape(values.shape)


def lower_unit(block, row_start, col_start):
    row_ids = row_start + lax.broadcasted_iota(jnp.int32, block.shape, 0)
    col_ids = col_start + lax.broadcasted_iota(jnp.int32, block.shape, 1)
    unit_ones = jnp.ones_like(block)
    unit_zeros = jnp.zeros_like(block)
    return jnp.where(col_ids < row_ids, block, jnp.where(col_ids == row_ids, unit_ones, unit_zeros))


def transposed_product(matrix, vector):
    return lax.dot_general(
        matrix, vector, (((0,), (0,)), ((), ())), preferred_element_type=jnp.float32
    )


def shards(
    child_inverse,
    child_lower,
    child_rhs,
    child_diag,
    child_off,
    child_pattern,
    child_pivots,
    child_map,
    root_inverse,
    root_rhs,
    root_diag,
    root_off,
    root_pattern,
):
    inverse_block = child_inverse[0]
    lower_block = child_lower[0]
    part_rows, part_cols = inverse_block.shape
    columns_rhs = child_rhs.shape[2]
    row_start = lax.axis_index("row") * part_rows
    col_start = lax.axis_index("col") * part_cols
    unit_child = lower_unit(inverse_block, row_start, col_start)
    forward_part = jnp.dot(unit_child, child_rhs[0], preferred_element_type=jnp.float32)
    forward_sum = lax.psum(forward_part, "col")
    live_rows = row_start + jnp.arange(part_rows, dtype=jnp.int32) < child_pivots[0]
    solved = jnp.where(live_rows[:, None], forward_sum, jnp.float32(0.0)).astype(jnp.bfloat16)
    scaled = pivot_solve(solved.astype(jnp.float32), child_diag[0], child_off[0], child_pattern[0])
    contrib_part = transposed_product(lower_block, solved)
    contrib = lax.psum(contrib_part, "row")
    sent_width = contrib.shape[1]
    local_map = child_map[0]
    block_rows = root_rhs.shape[0]
    targets = lax.axis_size("team") * lax.axis_size("col")
    capacity = 2 * local_map.shape[0] // targets
    owner = local_map // block_rows
    offset = local_map % block_rows
    onehot = (owner[:, None] == jnp.arange(targets, dtype=jnp.int32)[None, :]).astype(jnp.int32)
    ranks = jnp.sum((jnp.cumsum(onehot, axis=0) - 1) * onehot, axis=1)
    send_values = (
        jnp.zeros((targets, capacity, sent_width), jnp.float32).at[owner, ranks].set(contrib)
    )
    send_index = jnp.full((targets, capacity), block_rows, jnp.int32).at[owner, ranks].set(offset)
    got_values, got_index = (
        lax.all_to_all(send_values, ("team", "col"), split_axis=0, concat_axis=0, tiled=True),
        lax.all_to_all(send_index, ("team", "col"), split_axis=0, concat_axis=0, tiled=True),
    )
    assembled = (
        jnp.zeros((block_rows, sent_width), jnp.float32)
        .at[got_index.reshape(-1)]
        .add(got_values.reshape(-1, sent_width), mode="drop")
    )
    updated = (root_rhs.astype(jnp.float32) - assembled).astype(jnp.bfloat16)
    root_rows = root_inverse.shape[0]
    unit_root = lower_unit(
        root_inverse,
        lax.axis_index("row") * root_rows,
        lax.axis_index(("team", "col")) * block_rows,
    )
    root_part = jnp.dot(unit_root, updated, preferred_element_type=jnp.float32)
    root_forward = lax.psum(root_part, ("team", "col"))
    root_scaled = pivot_solve(root_forward, root_diag, root_off, root_pattern).astype(jnp.bfloat16)
    back_part = transposed_product(unit_root, root_scaled)
    root_solution = lax.psum(back_part, "row")
    root_rounded = root_solution.astype(jnp.bfloat16)
    initial = jnp.zeros((local_map.shape[0], columns_rhs), jnp.bfloat16)
    piece = lax.all_gather(root_rounded, ("team", "col"), axis=0, tiled=True)
    inside = (local_map >= 0) & (local_map < piece.shape[0])
    picked = jnp.take(piece, jnp.clip(local_map, 0, piece.shape[0] - 1), axis=0)
    fetched = jnp.where(inside[:, None], picked, initial)
    back_child = jnp.dot(lower_block, fetched, preferred_element_type=jnp.float32)
    back_sum = lax.psum(back_child, "col")
    residual = jnp.where(live_rows[:, None], scaled - back_sum, jnp.float32(0.0)).astype(
        jnp.bfloat16
    )
    child_part = transposed_product(unit_child, residual)
    child_solution = lax.psum(child_part, "row")
    return (child_solution[None], root_solution)


def solution(mesh):
    return jax.shard_map(
        shards,
        mesh=mesh,
        in_specs=(
            P("team", "row", "col"),
            P("team", "row", "col"),
            P("team", "col", None),
            P("team", "row"),
            P("team", "row"),
            P("team", "row"),
            P("team"),
            P("team", "col"),
            P("row", ("team", "col")),
            P(("team", "col"), None),
            P("row"),
            P("row"),
            P("row"),
        ),
        out_specs=(P("team", "col", None), P(("team", "col"), None)),
        check_vma=False,
    )
```

profile of v0, /device:TPU:2, one launch (start us, length us, event | category | flops | bytes accessed | tf_op | source)
XLA Modules:
  0.0 643.5 jit_solution(12600435542220784757)
XLA Ops:
  7.2 4.0 fusion.2
  11.2 53.3 %all-reduce.16 = bf16[1024,256]{1,0:T(8,128)(2,1)S(1)} all-reduce(f32[1024,256]{1,0:T(8,128)} %fusion.2), channel_id=1, replica_groups=mesh['team'=4,'row'=8,'col'=8] {'col'}, use_global_device_ids=true, to_apply=%region_0.1 | all-reduce | flops 262144 | bytes 1572864 | tf_op jit(solution)/shard_map/psum | solution.py:56
  65.2 1.8 fusion.13
  67.1 9.0 %reduce-window.6 = s32[32,8,128]{2,1,0:T(8,128)S(1)} reduce-window(s32[32,8,128]{2,1,0:T(8,128)S(1)} %fusion.42, s32[]{:T(128)} %constant.44.clone.1), window={size=1x1x128 pad=0_0x0_0x127_0}, to_apply=%region_1.2 | reduce-window | flops 4161536 | bytes 262148 | tf_op jit(solution)/shard_map/reduce-window
  76.9 4.3 scatter_custom_fusion.1
  81.2 0.7 all_to_all.9
  81.9 5.1 all-to-all-start
  87.0 56.6 %all-reduce.7.cloned.1.call-done = f32[1024,256]{0,1:T(8,128)} async-done(((f32[1024,256]{0,1:T(8,128)}), f32[1024,256]{0,1:T(8,128)}) %all-reduce.7.cloned.1.call-update) | async-done | bytes 1048592 | tf_op jit(solution)/shard_map/psum | solution.py:61
  143.6 2.5 copy.19
  146.1 6.7 %scatter_custom_fusion.2 = f32[2048,256]{1,0:T(8,128)} fusion(s32[1024]{0:T(1024)S(1)} %broadcast_select_fusion, f32[1024,256]{1,0:T(8,128)} %copy.19, f32[]{:T(128)} %constant.42.clone.1), kind=kCustom, calls=%fused_computation.27 | custom fusion | bytes 2097664
  152.8 7.6 %all-to-all-start.1 = ((f32[32,64,256]{2,1,0:T(8,128)}), f32[32,64,256]{2,1,0:T(8,128)}, u32[]{:S(2)}, u32[]{:S(2)}) async-start(f32[32,64,256]{2,1,0:T(8,128)} %bitcast.76), calls=%async_computation.1 | async-start | bytes 4194304 | tf_op jit(solution)/shard_map/all_to_all | solution.py:76
  160.5 0.5 broadcast.381
  161.0 0.7 reduce.9
  161.8 24.6 %all-to-all-done.1 = f32[32,64,256]{2,1,0:T(8,128)} async-done(((f32[32,64,256]{2,1,0:T(8,128)}), f32[32,64,256]{2,1,0:T(8,128)}, u32[]{:S(2)}, u32[]{:S(2)}) %all-to-all-start.1) | async-done | bytes 2097184 | tf_op jit(solution)/shard_map/all_to_all | solution.py:76
  186.4 12.1 %scatter_custom_fusion = f32[512,256]{1,0:T(8,128)S(1)} fusion(s32[2048]{0:T(1024)S(1)} %bitcast.84, f32[2048,256]{1,0:T(8,128)} %bitcast.19, f32[]{:T(128)} %constant.42.clone.1), kind=kCustom, calls=%fused_computation.52 | custom fusion | flops 524288 | bytes 524800 | tf_op jit(solution)/shard_map/scatter-add | solution.py:82
  198.5 4.2 fusion.35
  202.7 0.2 all-reduce.11.cloned.1.call-start
  203.0 0.4 copy-done.4
  203.6 0.2 slice.55
  203.8 0.2 slice.52
  204.1 0.2 slice.53
  204.3 112.8 %all-reduce.9.cloned.1.call-done = f32[2048,256]{1,0:T(8,128)} async-done(((f32[2048,256]{1,0:T(8,128)}), f32[2048,256]{1,0:T(8,128)}) %all-reduce.9.cloned.1.call-update) | async-done | bytes 2097168 | tf_op jit(solution)/shard_map/psum | solution.py:92
  317.1 6.3 slice.51
  323.3 6.3 slice.54
  329.6 2.2 fusion.33
  331.8 2.0 copy.20
  333.9 2.3 convert_element_type.32
  336.1 4.1 fusion.43
  340.3 73.9 %all-reduce.11.cloned.1.call-done = f32[512,256]{1,0:T(8,128)} async-done(((f32[512,256]{1,0:T(8,128)}), f32[512,256]{1,0:T(8,128)}) %all-reduce.11.cloned.1.call-update) | async-done | bytes 524304 | tf_op jit(solution)/shard_map/psum | solution.py:95
  414.2 1.8 convert_element_type.33
  416.0 0.2 slice.42
  416.3 0.2 slice.47
  416.5 0.2 slice.44
  416.7 0.2 slice.45
  417.0 1.2 fusion.61
  418.1 55.7 %all-gather.2.cloned.1.call-done = bf16[16384,256]{1,0:T(8,128)(2,1)} async-done(((bf16[512,256]{1,0:T(8,128)(2,1)}), bf16[16384,256]{1,0:T(8,128)(2,1)}) %all-gather.2.cloned.1.call-update) | async-done | bytes 8388624 | tf_op jit(solution)/shard_map/all_gather | solution.py:98
  473.9 9.1 %gather_fusion = bf16[1024,256]{1,0:T(8,128)(2,1)} fusion(bf16[16384,256]{1,0:T(8,128)(2,1)} %all-gather.2.cloned.1.call-done, s32[1024]{0:T(1024)S(1)} %broadcast_clamp_fusion), kind=kCustom, calls=%fused_computation | custom fusion | bytes 1052672 | tf_op jit(solution)/shard_map/jit(_take)/gather | solution.py:100
  482.9 3.0 fusion.16
  486.1 2.1 slice.43
  488.2 2.1 slice.46
  490.2 1.5 divide_bitcast_fusion.1
  491.9 0.8 copy.16
  492.7 1.7 reshape.305
  494.4 59.1 %all-reduce.13.cloned.1.call-done = f32[1024,256]{1,0:T(8,128)} async-done(((f32[1024,256]{1,0:T(8,128)}), f32[1024,256]{1,0:T(8,128)}) %all-reduce.13.cloned.1.call-update) | async-done | bytes 1048592 | tf_op jit(solution)/shard_map/psum | solution.py:103
  553.4 4.7 fusion.19
  558.2 75.4 %all-reduce.15.cloned.1.call-done = f32[1,1024,256]{2,1,0:T(8,128)} async-done(((f32[1,1024,256]{2,1,0:T(8,128)}), f32[1,1024,256]{2,1,0:T(8,128)}) %all-reduce.15.cloned.1.call-update) | async-done | bytes 1048592 | tf_op jit(solution)/shard_map/psum | solution.py:108
  633.6 2.3 copy.31
  635.8 0.8 copy.32
  (64 shorter events, 1.6 us)
Async XLA Ops:
  7.2 58.0 %copy-start = (bf16[1,1024,1024]{2,1,0:T(8,128)(2,1)S(1)}, bf16[1,1024,1024]{2,1,0:T(8,128)(2,1)}, u32[]{:S(2)}) copy-start(bf16[1,1024,1024]{2,1,0:T(8,128)(2,1)} %param.14) | copy-start | bytes 6291460
  7.2 136.4 %all-reduce.7.cloned.1.call-start = ((), (), s32[]{:S(2)}) async-start(), calls=%async_computation.2 | async-start | bytes 2097152 | tf_op jit(solution)/shard_map/psum | solution.py:61
  65.2 1.8 copy-start.3
  67.0 9.7 %copy-start.11 = (s32[2]{0:T(128)S(1)}, s32[2]{0:T(128)}, u32[]{:S(2)}) copy-start(s32[2]{0:T(128)} %constant.101) | copy-start | bytes 28
  67.0 9.7 %copy-start.10 = (s32[2]{0:T(128)S(1)}, s32[2]{0:T(128)}, u32[]{:S(2)}) copy-start(s32[2]{0:T(128)} %constant.104) | copy-start | bytes 28
  81.9 70.9 %all-to-all-start = ((s32[32,1,64]{2,1,0:T(1,128)}), s32[32,1,64]{2,1,0:T(1,128)S(1)}, u32[]{:S(2)}, u32[]{:S(2)}) async-start(s32[32,1,64]{2,1,0:T(1,128)} %all_to_all.9), calls=%async_computation | async-start | bytes 32768 | tf_op jit(solution)/shard_map/all_to_all | solution.py:77
  152.8 45.7 %copy-start.12 = (bf16[512,256]{1,0:T(8,128)(2,1)S(1)}, bf16[512,256]{1,0:T(8,128)(2,1)}, u32[]{:S(2)}) copy-start(bf16[512,256]{1,0:T(8,128)(2,1)} %param.22) | copy-start | bytes 786436
  152.8 33.6 %all-to-all-start.1 = ((f32[32,64,256]{2,1,0:T(8,128)}), f32[32,64,256]{2,1,0:T(8,128)}, u32[]{:S(2)}, u32[]{:S(2)}) async-start(f32[32,64,256]{2,1,0:T(8,128)} %bitcast.76), calls=%async_computation.1 | async-start | bytes 4194304 | tf_op jit(solution)/shard_map/all_to_all | solution.py:76
  160.4 156.6 %all-reduce.9.cloned.1.call-start = ((), (), s32[]{:S(2)}) async-start(), calls=%async_computation.3 | async-start | bytes 4194304 | tf_op jit(solution)/shard_map/psum | solution.py:92
  202.7 0.7 copy-start.4
  202.7 1.1 copy-start.6
  202.7 1.3 copy-start.7
  202.7 211.4 %all-reduce.11.cloned.1.call-start = ((), (), s32[]{:S(2)}) async-start(), calls=%async_computation.4 | async-start | bytes 1048576 | tf_op jit(solution)/shard_map/psum | solution.py:95
  336.1 79.9 %copy-start.5 = (f32[1,1024]{1,0:T(1,128)S(1)}, f32[1,1024]{1,0:T(1,128)}, u32[]{:S(2)}) copy-start(f32[1,1024]{1,0:T(1,128)} %param.16) | copy-start | bytes 12292
  336.1 80.3 %copy-start.8 = (s32[1,1024]{1,0:T(1,128)S(1)}, s32[1,1024]{1,0:T(1,128)}, u32[]{:S(2)}) copy-start(s32[1,1024]{1,0:T(1,128)} %param.18) | copy-start | bytes 12292
  336.1 80.6 %copy-start.9 = (f32[1,1024]{1,0:T(1,128)S(1)}, f32[1,1024]{1,0:T(1,128)}, u32[]{:S(2)}) copy-start(f32[1,1024]{1,0:T(1,128)} %param.17) | copy-start | bytes 12292
  340.3 133.6 %all-gather.2.cloned.1.call-start = ((), (), s32[]{:S(2)}) async-start(), calls=%async_computation.5 | async-start | bytes 8650752 | tf_op jit(solution)/shard_map/all_gather | solution.py:98
  416.0 137.5 %all-reduce.13.cloned.1.call-start = ((), (), s32[]{:S(2)}) async-start(), calls=%async_computation.6 | async-start | bytes 2097152 | tf_op jit(solution)/shard_map/psum | solution.py:103
  482.9 3.1 copy-start.1
  486.0 147.6 %all-reduce.15.cloned.1.call-start = ((), (), s32[]{:S(2)}) async-start(), calls=%async_computation.7 | async-start | bytes 2097152 | tf_op jit(solution)/shard_map/psum | solution.py:108
  558.1 77.7 %copy-start.2 = (f32[512,256]{1,0:T(8,128)S(1)}, f32[512,256]{1,0:T(8,128)}, u32[]{:S(2)}) copy-start(f32[512,256]{1,0:T(8,128)} %all-reduce.11.cloned.1.call-done) | copy-start | bytes 1572868
Sparse Core Ops, SparseCore 0:
  67.2 76.4 all-reduce.6
  202.9 114.1 all-reduce.8
  340.4 73.7 all-reduce.10
  417.5 56.3 all-gather.1
  486.1 67.2 all-reduce.12
  558.3 75.2 all-reduce.14
where the time goes:
time: 645 us; the launch traced here: 643 us
  waiting for transfers between devices  458 us (71%)
  blocking collectives  53.3 us (8%)
  local copies, waits for them, and re-layouts  52.9 us (8%)
  other arithmetic  29.1 us (5%)
  matrix products  21.8 us (3%)
  between operations  15.1 us (2%)
  starting transfers between devices  13.1 us (2%)
    psum x1, waiting for transfers between devices, shards(): root_forward = lax.psum(root_part, ('team', 'col'))  113 us
    psum x1, waiting for transfers between devices, shards(): child_solution = lax.psum(child_part, 'row')  75.4 us
    psum x1, waiting for transfers between devices, shards(): root_solution = lax.psum(back_part, 'row')  73.9 us
    psum x1, waiting for transfers between devices, shards(): back_sum = lax.psum(back_child, 'col')  59.1 us
    psum x1, waiting for transfers between devices, shards(): contrib = lax.psum(contrib_part, 'row')  56.6 us
    all_gather x1, waiting for transfers between devices, shards(): piece = lax.all_gather(root_rounded, ('team', 'col'), axis=0, tiled=True)  55.7 us
    psum x1, blocking collectives, shards(): forward_sum = lax.psum(forward_part, 'col')  53.3 us
    all_to_all x1, waiting for transfers between devices, shards(): lax.all_to_all(send_values, ('team', 'col'), split_axis=0, concat_axis=0,...  24.6 us
  transfers between devices with their start and end apart: 8, of which 7 were waited for; matrix products, arithmetic and copies ran while one was open for 6% of the time, Pallas kernels for 0%

commit v1 on v0

v1 whole, which is shorter than its diff:
```python
import functools

import jax
import jax.numpy as jnp
from jax import lax
from jax.experimental import pallas as pl
from jax.experimental.pallas import tpu as pltpu
from jax.sharding import PartitionSpec as P

BF = jnp.bfloat16
F32 = jnp.float32
MESH = pl.DeviceIdType.MESH
CORES = 2
CAP = 64
TILE = 256
CHAINS = 2


def nn(a, b):
    return jnp.dot(a, b, preferred_element_type=F32)


def nt(a, b):
    return lax.dot_general(a, b, (((1,), (1,)), ((), ())), preferred_element_type=F32)


def body(dims, *refs):
    T, Z, Y, CR, CC, U, RB, RR, R, H = dims
    C = Y * CORES
    Q = T * C
    G = T * Y
    W = R // H
    NS = Q * CAP
    pc, pr, pz, pu = CR // C, RR // Q, RB // Z, CC // Z
    it = iter(refs)
    take = lambda n: [next(it) for _ in range(n)]
    inv_h, low_h, root_h, rhs_h, rrhs_h = take(5)
    cdiag, coff, cpat, rdiag, roff, rpat, cmap, piv = take(8)
    out_c, out_r = take(2)
    inv, invt, low, lst, ls, sel, root, roott, asm, asmt, ident, rhs, rrhs = take(13)
    slot, msend, mrecv, cfa, cfb, rfa, rfb, scaled = take(8)
    s1, r1, s2, r2, sol, s3, r3, s4, r4, upd = take(10)
    s6, r6, s6b, r6b, rsc, s8, r8, rs, s10, r10 = take(10)
    s11, r11, s11b, r11b, res, s13, r13, cs = take(8)
    in_sem, snd, rcv, ysem, msem = take(5)

    t = lax.axis_index("team")
    r = lax.axis_index("row")
    c = lax.axis_index("col")
    y = c // CORES
    k = c % CORES
    me = t * C + c
    sib = (t, r, y * CORES + (1 - k))

    def plane_id(q):
        return (t * 0 + q // C, r, q % C)

    def z_id(d):
        return (t, (r + d) % Z, c)

    def y_id(d):
        return (t, r, ((y + d) % Y) * CORES + k)

    def g_id(g):
        return (g // Y, r, (g % Y) * CORES + k)

    barrier = pltpu.get_barrier_semaphore()

    def greet_plane(d, carry):
        pl.semaphore_signal(barrier, inc=1, device_id=plane_id((me + d) % Q), device_id_type=MESH)
        return carry

    def greet_z(d, carry):
        pl.semaphore_signal(barrier, inc=1, device_id=z_id(d), device_id_type=MESH)
        return carry

    loads = [pltpu.make_async_copy(rhs_h, rhs, in_sem.at[0])]
    for kk in range(CORES):
        loads.append(pltpu.make_async_copy(inv_h.at[:, kk], inv.at[pl.ds(kk * Y, Y)], in_sem.at[1 + kk]))
    for kk in range(CORES):
        loads.append(pltpu.make_async_copy(low_h.at[:, kk], low.at[pl.ds(kk * Y, Y)], in_sem.at[3 + kk]))
    for kk in range(CORES):
        loads.append(pltpu.make_async_copy(root_h.at[:, kk], root.at[pl.ds(kk * G, G)], in_sem.at[5 + kk]))
    loads.append(pltpu.make_async_copy(rrhs_h, rrhs, in_sem.at[7]))
    for ld in loads:
        ld.start()
    lax.fori_loop(1, Q, greet_plane, 0)
    lax.fori_loop(1, Z, greet_z, 0)

    def send(src, dst, sem_s, sem_r, dev):
        pltpu.make_async_remote_copy(
            src_ref=src, dst_ref=dst, send_sem=sem_s, recv_sem=sem_r, device_id=dev, device_id_type=MESH
        ).start()

    def arrive(view, sem):
        pltpu.make_async_copy(view, view, sem).wait()

    pending = []

    def sent(view, sem):
        pending.append((view, sem))

    def cols(h):
        return pl.ds(h * W, W)

    def tiled(n, fn, tile=TILE):
        def step(i, carry):
            fn(pl.multiple_of(i * tile, tile))
            return carry

        lax.fori_loop(0, n // tile, step, 0)

    def mask_child():
        @pl.when(c * CC + CC > r * CR)
        def _():
            def step(p, carry):
                piece = (p % Y) * CORES + p // Y
                rows = r * CR + piece * pc + lax.broadcasted_iota(jnp.int32, (pc, CC), 0)
                colid = c * CC + lax.broadcasted_iota(jnp.int32, (pc, CC), 1)
                blk = inv[p].astype(F32)
                blk = jnp.where(colid < rows, blk, jnp.where(colid == rows, 1.0, 0.0))
                inv[p] = blk.astype(BF)
                return carry

            lax.fori_loop(0, C, step, 0)

    def mask_root():
        for kk in range(2):
            loads[5 + kk].wait()

        @pl.when(me * RB + RB > r * RR)
        def _():
            def step(p, carry):
                g = p % G
                piece = (g // Y) * C + (g % Y) * CORES + p // G
                rows = r * RR + piece * pr + lax.broadcasted_iota(jnp.int32, (pr, RB), 0)
                colid = me * RB + lax.broadcasted_iota(jnp.int32, (pr, RB), 1)
                blk = root[p].astype(F32)
                blk = jnp.where(colid < rows, blk, jnp.where(colid == rows, 1.0, 0.0))
                root[p] = blk.astype(BF)
                return carry

            lax.fori_loop(0, 2 * G, step, 0)

    def make_ident():
        a = lax.broadcasted_iota(jnp.int32, (TILE, TILE), 0)
        b = lax.broadcasted_iota(jnp.int32, (TILE, TILE), 1)
        ident[...] = jnp.where(a == b, 1.0, 0.0).astype(BF)

    def transpose_into(x, xt, m, n, per):
        mt = min(512, m)
        for j in range(n // TILE):

            def step(i, carry):
                blk = x[pl.ds(i * (mt // per), mt // per), :, pl.ds(j * TILE, TILE)].reshape(mt, TILE)
                xt[pl.ds(j * TILE, TILE), pl.ds(pl.multiple_of(i * mt, mt), mt)] = nt(ident[...], blk).astype(BF)
                return carry

            lax.fori_loop(0, m // mt, step, 0)

    def make_slots():
        a = lax.broadcasted_iota(jnp.int32, (128, 128), 0)
        b = lax.broadcasted_iota(jnp.int32, (128, 128), 1)
        tri = jnp.where(a <= b, 1.0, 0.0).astype(BF)
        own_id = lax.broadcasted_iota(jnp.int32, (Q, 128), 0)
        base = jnp.zeros((Q, 1), F32)
        for i in range(U // 128):
            m = jnp.broadcast_to(cmap[:, i * 128 : (i + 1) * 128], (Q, 128))
            owner = m // RB
            hot = jnp.where(owner == own_id, 1.0, 0.0)
            count = nn(hot.astype(BF), tri)
            rank = jnp.sum(hot * (count + base - 1.0), axis=0, keepdims=True)
            base = base + jnp.sum(hot, axis=1, keepdims=True)
            slot[:, i * 128 : (i + 1) * 128] = jnp.broadcast_to(
                owner[0:8] * CAP + rank.astype(jnp.int32), (8, 128)
            )

    def make_sel():
        off = cmap[...] % RB
        row = lax.broadcasted_iota(jnp.int32, (16, U), 0)
        offb = jnp.broadcast_to(off, (16, U))
        probe = jnp.where(row == 0, offb // 16, jnp.where(row == 1, offb % 16, 1))
        probe = jnp.where(row < 3, probe, 0).astype(F32).astype(BF)

        def step(i, carry):
            ids = i * TILE + lax.broadcasted_iota(jnp.int32, (TILE, U), 0)
            blk = jnp.where(ids == slot[0:1, :], 1.0, 0.0).astype(BF)
            sel[pl.ds(pl.multiple_of(i * TILE, TILE), TILE), :] = blk
            info = nt(probe, blk)
            val = jnp.where(info[2:3] > 0.5, info[0:1] * 16.0 + info[1:2], float(RB))
            for j in range(TILE // 128):
                msend[i * (TILE // 128) + j] = jnp.broadcast_to(val[:, j * 128 : (j + 1) * 128], (8, 128))
            return carry

        lax.fori_loop(0, NS // TILE, step, 0)

    def send_meta():
        def step(d, carry):
            q = (me + d) % Q
            send(msend.at[q // 2], mrecv.at[me], msem.at[0], msem.at[1], plane_id(q))
            return carry

        lax.fori_loop(1, Q, step, 0)
        sent(mrecv.at[pl.ds(0, Q - 1)], msem.at[0])
        mrecv[me] = msend[me // 2]

    def make_lst():
        for kk in range(2):
            loads[3 + kk].wait()

        def step(i, carry):
            at = pl.ds(pl.multiple_of(i * TILE, TILE), TILE)
            blk = sel[at, :]
            for j in range(CR // 512):
                part = low[pl.ds(j * (512 // pc), 512 // pc)].reshape(512, U)
                lst[at, j * 512 : (j + 1) * 512] = nt(blk, part).astype(BF)
            return carry

        lax.fori_loop(0, NS // TILE, step, 0)

    def make_ls():
        def step(i, carry):
            part = low[pl.ds(i * (TILE // pc), TILE // pc)].reshape(TILE, U)
            at = pl.ds(pl.multiple_of(i * TILE, TILE), TILE)
            for j in range(NS // 512):
                ls[at, j * 512 : (j + 1) * 512] = nt(part, sel[j * 512 : (j + 1) * 512, :]).astype(BF)
            return carry

        lax.fori_loop(0, CR // TILE, step, 0)

    def make_asm():
        arrive(mrecv.at[pl.ds(0, Q - 1)], msem.at[1])

        def step(j, carry):
            lane = lax.broadcasted_iota(jnp.int32, (8, 128), 1)
            a, b = mrecv[2 * j], mrecv[2 * j + 1]
            ar, br = pltpu.roll(a, 64, 1), pltpu.roll(b, 64, 1)
            first = jnp.where(lane < 64, a, br)
            second = jnp.where(lane < 64, ar, b)
            kf = k.astype(F32)
            val = first * (1.0 - kf) + second * kf
            ids = lax.broadcasted_iota(jnp.int32, (RB, 128), 0).astype(F32)
            blk = jnp.where(ids == val[0:1, :], 1.0, 0.0).astype(BF)
            asm[:, pl.ds(pl.multiple_of(j * 128, 128), 128)] = blk
            return carry

        lax.fori_loop(0, Q // 2, step, 0)

    def make_asmt():
        def step(i, carry):
            at = pl.multiple_of(i * TILE, TILE)
            asmt[pl.ds(at, TILE), :] = nt(ident[...], asm[:, pl.ds(at, TILE)]).astype(BF)
            return carry

        lax.fori_loop(0, NS // TILE, step, 0)

    def coefficients(dref, oref, pref, fa, fb, start, n):
        first = (start // 128) * 128
        lane = lax.broadcasted_iota(jnp.int32, (128, 128), 1)
        even = lane % 2 == 0
        for i in range(max(1, n // 128)):
            at = pl.ds(pl.multiple_of(first + i * 128, 128), 128)
            a = jnp.broadcast_to(dref[:, at], (128, 128))
            o = jnp.broadcast_to(oref[:, at], (128, 128))
            p = jnp.broadcast_to(pref[:, at], (128, 128))
            partner = jnp.where(even, pltpu.roll(a, 127, 1), pltpu.roll(a, 1, 1))
            coup = jnp.where(p == 1, o, 0.0)
            coup = jnp.where(even, coup, pltpu.roll(coup, 1, 1))
            det = a * partner - coup * coup
            fa[pl.ds(i * 128, 128), :] = (partner / det).T
            fb[pl.ds(i * 128, 128), :] = (-coup / det).T

    def pivot(v, fa, fb, start, n):
        at = pl.ds(0, n) if n >= 128 else pl.ds(pl.multiple_of(start % 128, n), n)
        a = jnp.concatenate([fa[at, :]] * (W // 128), axis=1)
        b = jnp.concatenate([fb[at, :]] * (W // 128), axis=1)
        even = lax.broadcasted_iota(jnp.int32, (n, W), 0) % 2 == 0
        partner = jnp.where(even, pltpu.roll(v, n - 1, 0), pltpu.roll(v, 1, 0))
        return a * v + b * partner

    def make_coefs():
        coefficients(cdiag, coff, cpat, cfa, cfb, c * pc, pc)
        coefficients(rdiag, roff, rpat, rfa, rfb, me * pr, pr)

    half = CR // 2

    def col_core_send(h, s_a, r_a, st):
        send(s_a.at[h, pl.ds((1 - k) * half, half)], r_a.at[h], snd.at[h, st], rcv.at[h, st], sib)
        sent(r_a.at[h], snd.at[h, st])

    def col_y_send(h, s_a, r_a, s_b, r_b, st):
        arrive(r_a.at[h], rcv.at[h, st])
        s_b[h] = (s_a[h, pl.ds(pl.multiple_of(k * half, half), half), :].astype(F32) + r_a[h].astype(F32)).astype(BF)
        for d in range(1, Y):
            p = (y + d) % Y
            send(s_b.at[h, pl.ds(p * pc, pc)], r_b.at[h, pl.ds((d - 1) * pc, pc)], snd.at[h, st + 1], rcv.at[h, st + 1], y_id(d))
        sent(r_b.at[h], snd.at[h, st + 1])

    def col_sum(h, s_b, r_b, st):
        arrive(r_b.at[h], rcv.at[h, st + 1])
        acc = s_b[h, pl.ds(pl.multiple_of(y * pc, pc), pc), :].astype(F32)
        for d in range(Y - 1):
            acc = acc + r_b[h, d * pc : (d + 1) * pc, :].astype(F32)
        return acc

    def col_gather(h, buf, value, st, ys):
        at = pl.ds(pl.multiple_of(k * half + y * pc, pc), pc)
        buf[h, at, :] = value
        for d in range(1, Y):
            send(buf.at[h, at], buf.at[h, at], snd.at[h, st], ysem.at[h, ys, d - 1], y_id(d))
        send(buf.at[h, at], buf.at[h, at], snd.at[h, st + 1], rcv.at[h, st + 1], sib)
        sent(buf.at[h, pl.ds(0, (Y - 1) * pc)], snd.at[h, st])
        sent(buf.at[h, pl.ds(0, half)], snd.at[h, st + 1])

    def col_forward(h, buf, st, ys):
        for d in (1, Y - 1, 2) if Y == 4 else range(1, Y):
            at = pl.ds(pl.multiple_of(k * half + ((y + Y - d) % Y) * pc, pc), pc)
            arrive(buf.at[h, at], ysem.at[h, ys, d - 1])
            send(buf.at[h, at], buf.at[h, at], snd.at[h, st + 1], rcv.at[h, st + 1], sib)

    def col_gathered(h, buf, st):
        arrive(buf.at[h, pl.ds(0, half)], rcv.at[h, st + 1])

    def z_scatter(h, s, rr, n, st):
        def step(d, carry):
            to = (r + d) % Z
            send(s.at[h, pl.ds(to * n, n)], rr.at[h, pl.ds((d - 1) * n, n)], snd.at[h, st], rcv.at[h, st], z_id(d))
            return carry

        lax.fori_loop(1, Z, step, 0)
        sent(rr.at[h], snd.at[h, st])

    def z_sum(h, s, rr, n, st):
        arrive(rr.at[h], rcv.at[h, st])
        acc = s[h, pl.ds(pl.multiple_of(r * n, n), n), :].astype(F32)
        for d in range(Z - 1):
            acc = acc + rr[h, d * n : (d + 1) * n, :].astype(F32)
        return acc

    def z_gather(h, buf, value, n, st):
        at = pl.ds(pl.multiple_of(r * n, n), n)
        buf[h, at, :] = value

        def step(d, carry):
            send(buf.at[h, at], buf.at[h, at], snd.at[h, st], rcv.at[h, st], z_id(d))
            return carry

        lax.fori_loop(1, Z, step, 0)
        sent(buf.at[h, pl.ds(0, (Z - 1) * n)], snd.at[h, st])

    def z_gathered(h, buf, n, st):
        arrive(buf.at[h, pl.ds(0, (Z - 1) * n)], rcv.at[h, st])

    def exchange(h, mat, vec, s, rr, st):
        per = TILE // CAP
        groups = NS // TILE

        def step(i, carry):
            g = (me // per + 1 + i) % groups
            at = pl.multiple_of(g * TILE, TILE)
            s[h, pl.ds(at, TILE), :] = nn(mat[pl.ds(at, TILE), :], vec[h]).astype(BF)
            for j in range(per):
                q = g * per + j

                @pl.when(q != me)
                def _():
                    send(s.at[h, pl.ds(q * CAP, CAP)], rr.at[h, pl.ds(me * CAP, CAP)], snd.at[h, st], rcv.at[h, st], plane_id(q))

            return carry

        lax.fori_loop(0, groups, step, 0)
        sent(rr.at[h, pl.ds(0, NS - CAP)], snd.at[h, st])
        at = pl.ds(pl.multiple_of(me * CAP, CAP), CAP)
        rr[h, at, :] = s[h, at, :]

    def exchanged(h, rr, st):
        arrive(rr.at[h, pl.ds(0, NS - CAP)], rcv.at[h, st])

    def live(h):
        rows = r * CR + c * pc + lax.broadcasted_iota(jnp.int32, (pc, W), 0)
        return rows < piv[0]

    def a1(h):
        def fn(i):
            p = i // pc
            tile = inv[pl.ds(p, TILE // pc)].reshape(TILE, CC)
            s1[h, pl.ds(i, TILE), :] = nn(tile, rhs[:, h * W : (h + 1) * W]).astype(BF)

        tiled(CR, fn)

    def a2(h):
        col_core_send(h, s1, r1, 0)

    def b(h):
        col_y_send(h, s1, r1, s2, r2, 0)

    def cc(h):
        acc = col_sum(h, s2, r2, 0)
        solved = jnp.where(live(h), acc, 0.0).astype(BF)
        col_gather(h, sol, solved, 2, 0)
        scaled[h] = pivot(solved.astype(F32), cfa, cfb, c * pc, pc)

    def d(h):
        col_forward(h, sol, 2, 0)

    def e(h):
        col_gathered(h, sol, 2)
        exchange(h, lst, sol, s3, r3, 4)

    def f(h):
        exchanged(h, r3, 4)

        def fn(i):
            s4[h, pl.ds(i, TILE), :] = nn(asm[pl.ds(i, TILE), :], r3[h]).astype(BF)

        tiled(RB, fn)
        z_scatter(h, s4, r4, pz, 5)

    def g(h):
        acc = z_sum(h, s4, r4, pz, 5)
        mine = rrhs[pl.ds(pl.multiple_of(r * pz, pz), pz), h * W : (h + 1) * W].astype(F32)
        z_gather(h, upd, (mine - acc).astype(BF), pz, 6)

    def hh(h):
        z_gathered(h, upd, pz, 6)

        def fn(i):
            tile = root[pl.ds(i // pr, TILE // pr)].reshape(TILE, RB)
            s6[h, pl.ds(i, TILE), :] = nn(tile, upd[h]).astype(BF)

        tiled(RR, fn)
        rh = RR // 2
        send(s6.at[h, pl.ds((1 - k) * rh, rh)], r6.at[h], snd.at[h, 7], rcv.at[h, 7], sib)
        sent(r6.at[h], snd.at[h, 7])

    def i_(h):
        arrive(r6.at[h], rcv.at[h, 7])
        rh = RR // 2
        gi = t * Y + y

        def step(j, carry):
            p = (gi + 1 + j) % G
            at = pl.ds(pl.multiple_of(p * pr, pr), pr)
            mine = pl.ds(pl.multiple_of(k * rh + p * pr, pr), pr)
            s6b[h, at, :] = (s6[h, mine, :].astype(F32) + r6[h, at, :].astype(F32)).astype(BF)

            @pl.when(p != gi)
            def _():
                send(s6b.at[h, at], r6b.at[h, pl.ds(j * pr, pr)], snd.at[h, 8], rcv.at[h, 8], g_id(p))

            return carry

        lax.fori_loop(0, G, step, 0)
        sent(r6b.at[h], snd.at[h, 8])

    def j_(h):
        arrive(r6b.at[h], rcv.at[h, 8])
        gi = t * Y + y
        acc = s6b[h, pl.ds(pl.multiple_of(gi * pr, pr), pr), :].astype(F32)
        for n in range(G - 1):
            acc = acc + r6b[h, n * pr : (n + 1) * pr, :].astype(F32)
        value = pivot(acc, rfa, rfb, me * pr, pr).astype(BF)
        at = pl.ds(pl.multiple_of((k * G + gi) * pr, pr), pr)
        rsc[h, at, :] = value

        def step(n, carry):
            send(rsc.at[h, at], rsc.at[h, at], snd.at[h, 9], rcv.at[h, 9], g_id((gi + n) % G))
            return carry

        lax.fori_loop(1, G, step, 0)
        sent(rsc.at[h, pl.ds(0, (G - 1) * pr)], snd.at[h, 9])

    def k_(h):
        rh = RR // 2
        arrive(rsc.at[h, pl.ds(0, (G - 1) * pr)], rcv.at[h, 9])
        mine = pl.ds(k * rh, rh)
        send(rsc.at[h, mine], rsc.at[h, mine], snd.at[h, 10], rcv.at[h, 10], sib)
        sent(rsc.at[h, pl.ds(0, rh)], snd.at[h, 10])

    def l_(h):
        arrive(rsc.at[h, pl.ds(0, RR // 2)], rcv.at[h, 10])

        def fn(i):
            s8[h, pl.ds(i, TILE), :] = nn(roott[pl.ds(i, TILE), :], rsc[h]).astype(BF)

        tiled(RB, fn)
        z_scatter(h, s8, r8, pz, 11)

    def m_(h):
        z_gather(h, rs, z_sum(h, s8, r8, pz, 11).astype(BF), pz, 12)

    def n_(h):
        z_gathered(h, rs, pz, 12)
        exchange(h, asmt, rs, s10, r10, 13)
        out_r[:, h * W : (h + 1) * W] = rs[h]

    def o_(h):
        exchanged(h, r10, 13)

        def fn(i):
            s11[h, pl.ds(i, TILE), :] = nn(ls[pl.ds(i, TILE), :], r10[h]).astype(BF)

        tiled(CR, fn)
        col_core_send(h, s11, r11, 14)

    def p_(h):
        col_y_send(h, s11, r11, s11b, r11b, 14)

    def q_(h):
        acc = col_sum(h, s11b, r11b, 14)
        value = jnp.where(live(h), scaled[h] - acc, 0.0).astype(BF)
        col_gather(h, res, value, 16, 1)

    def r_(h):
        col_forward(h, res, 16, 1)

    def s_(h):
        col_gathered(h, res, 16)

        def fn(i):
            s13[h, pl.ds(i, TILE), :] = nn(invt[pl.ds(i, TILE), :], res[h]).astype(BF)

        tiled(CC, fn)
        z_scatter(h, s13, r13, pu, 18)

    def t_(h):
        z_gather(h, cs, z_sum(h, s13, r13, pu, 18).astype(BF), pu, 19)

    def u_(h):
        z_gathered(h, cs, pu, 19)
        out_c[:, h * W : (h + 1) * W] = cs[h]

    for n in range(3):
        loads[n].wait()
    mask_child()
    for h in range(H):
        a1(h)
    pl.semaphore_wait(barrier, Q - 1 + Z - 1)
    plan = [
        (a2, [make_slots, make_sel]),
        (b, [send_meta, make_coefs, make_lst]),
        (cc, [make_ident]),
        (d, []),
        (e, [make_asm, mask_root]),
        (f, [make_ls]),
        (g, [lambda: transpose_into(root, roott, RR, RB, pr)]),
        (hh, []),
        (i_, [make_asmt]),
        (j_, [lambda: transpose_into(inv, invt, CR, CC, pc)]),
        (k_, []), (l_, []), (m_, []), (n_, []), (o_, []), (p_, []), (q_, []), (r_, []), (s_, []), (t_, []), (u_, []),
    ]
    for stage, background in plan:
        if stage is g:
            loads[7].wait()
        for h in range(H):
            stage(h)
        for work in background:
            work()
    for view, sem in pending:
        arrive(view, sem)


def shards(dims, *args):
    (child_inverse, child_lower, child_rhs, child_diag, child_off, child_pattern, child_pivots, child_map,
     root_inverse, root_rhs, root_diag, root_off, root_pattern) = args
    T, Z, Y, CR, CC, U, RB, RR, R, H = dims
    C, Q, G, W = Y * CORES, T * Y * CORES, T * Y, R // H
    NS = Q * CAP
    pc, pr, pz, pu = CR // C, RR // Q, RB // Z, CC // Z

    def chain(rows):
        return pltpu.VMEM((H, rows, W), BF)

    vm = lambda *shape: pltpu.VMEM(shape, BF)
    fm = lambda *shape: pltpu.VMEM(shape, F32)
    half = CR // 2
    scratch = [
        vm(C, pc, CC), vm(CC, CR), vm(C, pc, U), vm(NS, CR), vm(CR, NS), vm(NS, U), vm(Q, pr, RB), vm(RB, RR),
        vm(RB, NS), vm(NS, RB), vm(TILE, TILE), vm(CC, R), vm(RB, R),
        pltpu.VMEM((8, U), jnp.int32), fm(Q // 2, 8, 128), fm(Q, 8, 128),
        fm(max(pc, 128), 128), fm(max(pc, 128), 128), fm(max(pr, 128), 128), fm(max(pr, 128), 128), fm(H, pc, W),
        chain(CR), chain(half), chain(half), chain((Y - 1) * pc), chain(CR), chain(NS), chain(NS), chain(RB),
        chain((Z - 1) * pz), chain(RB),
        chain(RR), chain(RR // 2), chain(RR // 2), chain((G - 1) * pr), chain(RR), chain(RB), chain((Z - 1) * pz),
        chain(RB), chain(NS), chain(NS),
        chain(CR), chain(half), chain(half), chain((Y - 1) * pc), chain(CR), chain(CC), chain((Z - 1) * pu), chain(CC),
        pltpu.SemaphoreType.DMA((8,)), pltpu.SemaphoreType.DMA((H, 20)), pltpu.SemaphoreType.DMA((H, 20)),
        pltpu.SemaphoreType.DMA((H, 2, Y - 1)), pltpu.SemaphoreType.DMA((2,)),
    ]
    anyspec = pl.BlockSpec(memory_space=pl.ANY)
    vspec = pl.BlockSpec(memory_space=pltpu.VMEM)
    flops = 2 * R * (2 * CR * CC + 2 * NS * CR + 2 * RB * NS + 2 * RR * RB)
    child, rooted = pl.pallas_call(
        functools.partial(body, dims),
        name="substitution",
        out_shape=(jax.ShapeDtypeStruct((CC, R), BF), jax.ShapeDtypeStruct((RB, R), BF)),
        in_specs=[anyspec] * 5 + [vspec] * 7 + [pl.BlockSpec(memory_space=pltpu.SMEM)],
        out_specs=(vspec, vspec),
        scratch_shapes=scratch,
        cost_estimate=pl.CostEstimate(flops=flops, bytes_accessed=8 << 20, transcendentals=0),
        compiler_params=pltpu.CompilerParams(collective_id=0, has_side_effects=True, vmem_limit_bytes=58 << 20),
    )(
        child_inverse.reshape(Y, CORES, pc, CC),
        child_lower.reshape(Y, CORES, pc, U),
        root_inverse.reshape(G, CORES, pr, RB),
        child_rhs.reshape(CC, R),
        root_rhs,
        child_diag.reshape(1, CR),
        child_off.reshape(1, CR),
        child_pattern.reshape(1, CR),
        root_diag.reshape(1, RR),
        root_off.reshape(1, RR),
        root_pattern.reshape(1, RR),
        child_map.reshape(1, U),
        child_pivots,
    )
    return (child.astype(F32)[None], rooted.astype(F32))


def solution(mesh):
    T, Z, C = mesh.shape["team"], mesh.shape["row"], mesh.shape["col"]

    def run(*args):
        pc_, uc = args[0].shape[1], args[1].shape[2]
        fr, R = args[9].shape
        dims = (T, Z, C // CORES, pc_ // Z, pc_ // C, uc // C, fr // (T * C), fr // Z, R, CHAINS)
        return jax.shard_map(
            functools.partial(shards, dims),
            mesh=mesh,
            in_specs=(
                P("team", "row", "col"),
                P("team", "row", "col"),
                P("team", "col", None),
                P("team", "row"),
                P("team", "row"),
                P("team", "row"),
                P("team"),
                P("team", "col"),
                P("row", ("team", "col")),
                P(("team", "col"), None),
                P("row"),
                P("row"),
                P("row"),
            ),
            out_specs=(P("team", "col", None), P(("team", "col"), None)),
            check_vma=False,
        )(*args)

    return run
```

time: 645 us -> 150 us (0.23)
  waiting for transfers between devices: 458 us -> 0 us
  Pallas kernels: 0 us -> 143 us
  blocking collectives: 53.3 us -> 0 us
  local copies, waits for them, and re-layouts: 52.9 us -> 0 us
  other arithmetic: 29.1 us -> 3.86 us
  matrix products: 21.8 us -> 0 us
  between operations: 15.1 us -> 1.29 us
  starting transfers between devices: 13.1 us -> 0 us
    psum x5 -> x0, waiting for transfers between devices: 378 us -> none  [the longest x1 113 us: shards(): root_forward = lax.psum(root_part, ('team', 'col'))]
    pallas_call x0 -> x1, Pallas kernels: none -> 143 us  [shards(): pl.pallas_call(functools.partial(body, dims), name='substitution', out_sh...]
    all_gather x1 -> x0, waiting for transfers between devices: 55.7 us -> none  [shards(): piece = lax.all_gather(root_rounded, ('team', 'col'), axis=0, tiled=True)]
    psum x1 -> x0, blocking collectives: 53.3 us -> none  [shards(): forward_sum = lax.psum(forward_part, 'col')]
    all_to_all x2 -> x0, waiting for transfers between devices: 24.6 us -> none  [the longest x1 24.6 us: shards(): lax.all_to_all(send_values, ('team', 'col'), split_axis=0, concat_axis=0,...]
    dot_general x6 -> x0, matrix products: 21.8 us -> none  [the longest x3 10.6 us: transposed_product(): lax.dot_general(matrix, vector, (((0,), (0,)), ((), ())), preferred_eleme...]
    slice x14 -> x0, local copies, waits for them, and re-layouts: 18.6 us -> none  [the longest x2 8.35 us: pivot_solve(): first_rows = values[0::2]]
    unnamed x30 -> x0, local copies, waits for them, and re-layouts: 14.5 us -> none
  transfers between devices with their start and end apart: 8 -> 0, of which waited for: 7 -> 0; matrix products, arithmetic and copies ran while one was open for 6% -> 0% of each run, Pallas kernels for 0% -> 0%
where the time goes in v1:
time: 150 us; the launch traced here: 148 us
  Pallas kernels  143 us (95%)
  other arithmetic  3.86 us (3%)
    pallas_call x1, Pallas kernels, shards(): pl.pallas_call(functools.partial(body, dims), name='substitution', out_sh...  143 us

profile of v1, /device:TPU:2, one launch (start us, length us, event | category | flops | bytes accessed | tf_op | source)
XLA Modules:
  0.0 147.8 jit_solution(17800536567604115983)
XLA Ops:
  1.3 142.6 %substitution.1 = (bf16[1024,256]{1,0:T(8,128)(2,1)}, bf16[512,256]{1,0:T(8,128)(2,1)}) custom-call(bf16[4,2,128,1024]{3,2,1,0:T(8,128)(2,1)} %bitcast.10, bf16[4,2,128,1024]{3,2,1,0:T(8,128)(2,1)} %bitcast.11, bf16[16,2,64,512]{3,2,1,0:T(8,128)(2,1)} %bitcast.12, bf16[1024,256]{1,0:T(8,128)(2,1)} %bitcast.13, bf16[512,256]{1,0:T(8,128)(2,1)} %refs_4_.1, ...), custom_call_target="tpu_custom_call" | custom-call | flops 5368709120 | bytes 8388608 | tf_op jit(solution)/shard_map/substitution/pallas_call | solution.py:593
  143.9 2.1 %bitcast_convert_fusion = f32[1,1024,256]{2,1,0:T(8,128)} fusion(bf16[1024,256]{1,0:T(8,128)(2,1)} %get-tuple-element.4), kind=kLoop, calls=%fused_computation | loop fusion | flops 262144 | bytes 1572864 | tf_op jit(solution)/shard_map/broadcast_in_dim | solution.py:617
  146.0 1.8 %convert_element_type.4 = f32[512,256]{1,0:T(8,128)} convert(bf16[512,256]{1,0:T(8,128)(2,1)} %get-tuple-element.5) | non-fusion elementwise | flops 131072 | bytes 786432 | tf_op jit(solution)/shard_map/convert_element_type | solution.py:617

commit v2 on v1

--- a/solution.py
+++ b/solution.py
@@ -13,7 +13,17 @@
 CORES = 2
 CAP = 64
 TILE = 256
+MT = 512
+XT = 256
+UNROLL = False
 CHAINS = 2
+ORDER = ["a0", "a1", "sel", "b0", "b1", "meta", "lst0", "c0", "c1", "ident", "lst1", "d0", "d1", "e0", "e1"]
+ORDER += ["asm", "f0", "rrhs", "mask", "coefs", "f1", "roott", "g0", "g1", "h0", "i0", "h1", "i1", "j0", "asmt"]
+ORDER += ["j1", "k0", "l0", "k1", "l1", "ls0", "m0", "ls1", "m1", "n0", "n1", "invt", "o0", "p0", "o1", "q0", "p1"]
+ORDER += ["r0", "q1", "s0", "r1", "s1", "S0", "S1", "t0", "t1", "T0", "T1", "u0", "u1"]
+TREE = True
+RST = False
+OUT = pltpu.VMEM
 
 
 def nn(a, b):
@@ -35,14 +45,16 @@
     it = iter(refs)
     take = lambda n: [next(it) for _ in range(n)]
     inv_h, low_h, root_h, rhs_h, rrhs_h = take(5)
-    cdiag, coff, cpat, rdiag, roff, rpat, cmap, piv = take(8)
+    small_h = take(8)
     out_c, out_r = take(2)
     inv, invt, low, lst, ls, sel, root, roott, asm, asmt, ident, rhs, rrhs = take(13)
     slot, msend, mrecv, cfa, cfb, rfa, rfb, scaled = take(8)
     s1, r1, s2, r2, sol, s3, r3, s4, r4, upd = take(10)
     s6, r6, s6b, r6b, rsc, s8, r8, rs, s10, r10 = take(10)
-    s11, r11, s11b, r11b, res, s13, r13, cs = take(8)
-    in_sem, snd, rcv, ysem, msem = take(5)
+    s11, r11, s11b, r11b, res, s13, r13, mid, cs = take(9)
+    small = take(8)
+    cdiag, coff, cpat, rdiag, roff, rpat, cmap, piv = small
+    in_sem, small_sem, snd, rcv, ysem, zsem, msem = take(7)
 
     t = lax.axis_index("team")
     r = lax.axis_index("row")
@@ -82,10 +94,14 @@
     for kk in range(CORES):
         loads.append(pltpu.make_async_copy(root_h.at[:, kk], root.at[pl.ds(kk * G, G)], in_sem.at[5 + kk]))
     loads.append(pltpu.make_async_copy(rrhs_h, rrhs, in_sem.at[7]))
-    for ld in loads:
+    small_loads = [pltpu.make_async_copy(a, b, small_sem.at[n]) for n, (a, b) in enumerate(zip(small_h, small))]
+    small_loads[6].start()
+    for ld in loads[:3]:
         ld.start()
-    lax.fori_loop(1, Q, greet_plane, 0)
-    lax.fori_loop(1, Z, greet_z, 0)
+    lax.fori_loop(1, Q, greet_plane, 0, unroll=UNROLL)
+    lax.fori_loop(1, Z, greet_z, 0, unroll=UNROLL)
+    for ld in small_loads[7:] + loads[3:] + small_loads[:6]:
+        ld.start()
 
     def send(src, dst, sem_s, sem_r, dev):
         pltpu.make_async_remote_copy(
@@ -103,7 +119,19 @@
     def cols(h):
         return pl.ds(h * W, W)
 
-    def tiled(n, fn, tile=TILE):
+    def halves(n, fn, push):
+        def step(i, carry):
+            fn(pl.multiple_of(((1 - k) * (n // 2 // MT) + i) % (n // MT) * MT, MT))
+
+            @pl.when(i == n // 2 // MT - 1)
+            def _():
+                push()
+
+            return carry
+
+        lax.fori_loop(0, n // MT, step, 0)
+
+    def tiled(n, fn, tile=MT):
         def step(i, carry):
             fn(pl.multiple_of(i * tile, tile))
             return carry
@@ -111,18 +139,25 @@
         lax.fori_loop(0, n // tile, step, 0)
 
     def mask_child():
-        @pl.when(c * CC + CC > r * CR)
+        @pl.when(c > r)
         def _():
             def step(p, carry):
-                piece = (p % Y) * CORES + p // Y
-                rows = r * CR + piece * pc + lax.broadcasted_iota(jnp.int32, (pc, CC), 0)
-                colid = c * CC + lax.broadcasted_iota(jnp.int32, (pc, CC), 1)
-                blk = inv[p].astype(F32)
+                inv[p] = jnp.zeros((pc, CC), BF)
+                return carry
+
+            lax.fori_loop(0, C, step, 0)
+
+        @pl.when(c == r)
+        def _():
+            rows = lax.broadcasted_iota(jnp.int32, (pc, pc), 0)
+            colid = lax.broadcasted_iota(jnp.int32, (pc, pc), 1)
+            for p in range(C):
+                at = ((p % Y) * CORES + p // Y) * pc
+                blk = inv[p, :, at : at + pc].astype(F32)
                 blk = jnp.where(colid < rows, blk, jnp.where(colid == rows, 1.0, 0.0))
-                inv[p] = blk.astype(BF)
-                return carry
-
-            lax.fori_loop(0, C, step, 0)
+                inv[p, :, at : at + pc] = blk.astype(BF)
+                if at + pc < CC:
+                    inv[p, :, at + pc :] = jnp.zeros((pc, CC - at - pc), BF)
 
     def mask_root():
         for kk in range(2):
@@ -204,9 +239,10 @@
         sent(mrecv.at[pl.ds(0, Q - 1)], msem.at[0])
         mrecv[me] = msend[me // 2]
 
-    def make_lst():
-        for kk in range(2):
-            loads[3 + kk].wait()
+    def make_lst(part_no):
+        if part_no == 0:
+            for kk in range(2):
+                loads[3 + kk].wait()
 
         def step(i, carry):
             at = pl.ds(pl.multiple_of(i * TILE, TILE), TILE)
@@ -216,9 +252,10 @@
                 lst[at, j * 512 : (j + 1) * 512] = nt(blk, part).astype(BF)
             return carry
 
-        lax.fori_loop(0, NS // TILE, step, 0)
-
-    def make_ls():
+        count = NS // TILE // 2
+        lax.fori_loop(part_no * count, (part_no + 1) * count, step, 0)
+
+    def make_ls(part_no):
         def step(i, carry):
             part = low[pl.ds(i * (TILE // pc), TILE // pc)].reshape(TILE, U)
             at = pl.ds(pl.multiple_of(i * TILE, TILE), TILE)
@@ -226,7 +263,8 @@
                 ls[at, j * 512 : (j + 1) * 512] = nt(part, sel[j * 512 : (j + 1) * 512, :]).astype(BF)
             return carry
 
-        lax.fori_loop(0, CR // TILE, step, 0)
+        count = CR // TILE // 2
+        lax.fori_loop(part_no * count, (part_no + 1) * count, step, 0)
 
     def make_asm():
         arrive(mrecv.at[pl.ds(0, Q - 1)], msem.at[1])
@@ -286,7 +324,6 @@
 
     def col_core_send(h, s_a, r_a, st):
         send(s_a.at[h, pl.ds((1 - k) * half, half)], r_a.at[h], snd.at[h, st], rcv.at[h, st], sib)
-        sent(r_a.at[h], snd.at[h, st])
 
     def col_y_send(h, s_a, r_a, s_b, r_b, st):
         arrive(r_a.at[h], rcv.at[h, st])
@@ -321,13 +358,17 @@
     def col_gathered(h, buf, st):
         arrive(buf.at[h, pl.ds(0, half)], rcv.at[h, st + 1])
 
+    def far(i):
+        return Z // 2 + (1 - 2 * (i % 2)) * ((i + 1) // 2)
+
     def z_scatter(h, s, rr, n, st):
-        def step(d, carry):
+        def step(i, carry):
+            d = far(i)
             to = (r + d) % Z
             send(s.at[h, pl.ds(to * n, n)], rr.at[h, pl.ds((d - 1) * n, n)], snd.at[h, st], rcv.at[h, st], z_id(d))
             return carry
 
-        lax.fori_loop(1, Z, step, 0)
+        lax.fori_loop(0, Z - 1, step, 0, unroll=UNROLL)
         sent(rr.at[h], snd.at[h, st])
 
     def z_sum(h, s, rr, n, st):
@@ -341,24 +382,72 @@
         at = pl.ds(pl.multiple_of(r * n, n), n)
         buf[h, at, :] = value
 
-        def step(d, carry):
-            send(buf.at[h, at], buf.at[h, at], snd.at[h, st], rcv.at[h, st], z_id(d))
-            return carry
-
-        lax.fori_loop(1, Z, step, 0)
+        def step(i, carry):
+            send(buf.at[h, at], buf.at[h, at], snd.at[h, st], rcv.at[h, st], z_id(far(i)))
+            return carry
+
+        lax.fori_loop(0, Z - 1, step, 0, unroll=UNROLL)
         sent(buf.at[h, pl.ds(0, (Z - 1) * n)], snd.at[h, st])
 
     def z_gathered(h, buf, n, st):
         arrive(buf.at[h, pl.ds(0, (Z - 1) * n)], rcv.at[h, st])
 
+    def z_tree_scatter(h, s, mid, rr, n, st):
+        def part(to):
+            return s.at[h, pl.ds(((r + to) % Z) * n, n)]
+
+        for i, (to, via) in enumerate(((3, 1), (Z - 3, Z - 1), (4, (2, Z - 2)[h % 2]))):
+            sem = zsem.at[h, 2 + (i if i < 2 else h % 2)]
+            send(part(to), mid.at[h, pl.ds(i * n, n)], snd.at[h, st], sem, z_id(via))
+        for i, to in enumerate((1, Z - 1)):
+            send(part(to), rr.at[h, pl.ds(i * n, n)], snd.at[h, st], rcv.at[h, st], z_id(to))
+        sent(s.at[h, pl.ds(0, 5 * n)], snd.at[h, st])
+
+    def z_tree_pass(h, s, mid, rr, n, st):
+        for i, to in enumerate((2, Z - 2)):
+            both = i == h % 2
+            view = mid.at[h, pl.ds(0, (2 if both else 1) * n)]
+            arrive(view, zsem.at[h, 2 + i])
+            at = pl.ds(pl.multiple_of(((r + to) % Z) * n, n), n)
+            acc = s[h, at, :].astype(F32) + mid[h, i * n : (i + 1) * n, :].astype(F32)
+            if both:
+                acc = acc + mid[h, 2 * n : 3 * n, :].astype(F32)
+            s[h, at, :] = acc.astype(BF)
+            send(s.at[h, at], rr.at[h, pl.ds((2 + i) * n, n)], snd.at[h, st + 1], rcv.at[h, st], z_id(to))
+        sent(s.at[h, pl.ds(0, 2 * n)], snd.at[h, st + 1])
+
+    def z_tree_sum(h, s, rr, n, st):
+        arrive(rr.at[h, pl.ds(0, 4 * n)], rcv.at[h, st])
+        acc = s[h, pl.ds(pl.multiple_of(r * n, n), n), :].astype(F32)
+        for d in range(4):
+            acc = acc + rr[h, d * n : (d + 1) * n, :].astype(F32)
+        return acc
+
+    def z_tree(h, buf, value, n, st):
+        at = pl.ds(pl.multiple_of(r * n, n), n)
+        buf[h, at, :] = value
+        for i, d in enumerate((2, Z - 2)):
+            send(buf.at[h, at], buf.at[h, at], snd.at[h, st], zsem.at[h, i], z_id(d))
+        for d in (1, Z - 1):
+            send(buf.at[h, at], buf.at[h, at], snd.at[h, st], rcv.at[h, st], z_id(d))
+        sent(buf.at[h, pl.ds(0, (Z - 1) * n)], snd.at[h, st])
+
+    def z_tree_forward(h, buf, n, st):
+        for i, d in enumerate((2, Z - 2)):
+            at = pl.ds(pl.multiple_of(((r + Z - d) % Z) * n, n), n)
+            arrive(buf.at[h, at], zsem.at[h, i])
+            if i == h % 2:
+                send(buf.at[h, at], buf.at[h, at], snd.at[h, st], rcv.at[h, st], z_id(d))
+            send(buf.at[h, at], buf.at[h, at], snd.at[h, st], rcv.at[h, st], z_id((1, Z - 1)[i]))
+
     def exchange(h, mat, vec, s, rr, st):
-        per = TILE // CAP
-        groups = NS // TILE
+        per = XT // CAP
+        groups = NS // XT
 
         def step(i, carry):
             g = (me // per + 1 + i) % groups
-            at = pl.multiple_of(g * TILE, TILE)
-            s[h, pl.ds(at, TILE), :] = nn(mat[pl.ds(at, TILE), :], vec[h]).astype(BF)
+            at = pl.multiple_of(g * XT, XT)
+            s[h, pl.ds(at, XT), :] = nn(mat[pl.ds(at, XT), :], vec[h]).astype(BF)
             for j in range(per):
                 q = g * per + j
 
@@ -378,18 +467,15 @@
 
     def live(h):
         rows = r * CR + c * pc + lax.broadcasted_iota(jnp.int32, (pc, W), 0)
-        return rows < piv[0]
+        return rows < piv[...]
 
     def a1(h):
         def fn(i):
             p = i // pc
-            tile = inv[pl.ds(p, TILE // pc)].reshape(TILE, CC)
-            s1[h, pl.ds(i, TILE), :] = nn(tile, rhs[:, h * W : (h + 1) * W]).astype(BF)
-
-        tiled(CR, fn)
-
-    def a2(h):
-        col_core_send(h, s1, r1, 0)
+            tile = inv[pl.ds(p, MT // pc)].reshape(MT, CC)
+            s1[h, pl.ds(i, MT), :] = nn(tile, rhs[:, h * W : (h + 1) * W]).astype(BF)
+
+        return fn
 
     def b(h):
         col_y_send(h, s1, r1, s2, r2, 0)
@@ -398,7 +484,6 @@
         acc = col_sum(h, s2, r2, 0)
         solved = jnp.where(live(h), acc, 0.0).astype(BF)
         col_gather(h, sol, solved, 2, 0)
-        scaled[h] = pivot(solved.astype(F32), cfa, cfb, c * pc, pc)
 
     def d(h):
         col_forward(h, sol, 2, 0)
@@ -411,7 +496,7 @@
         exchanged(h, r3, 4)
 
         def fn(i):
-            s4[h, pl.ds(i, TILE), :] = nn(asm[pl.ds(i, TILE), :], r3[h]).astype(BF)
+            s4[h, pl.ds(i, MT), :] = nn(asm[pl.ds(i, MT), :], r3[h]).astype(BF)
 
         tiled(RB, fn)
         z_scatter(h, s4, r4, pz, 5)
@@ -425,12 +510,11 @@
         z_gathered(h, upd, pz, 6)
 
         def fn(i):
-            tile = root[pl.ds(i // pr, TILE // pr)].reshape(TILE, RB)
-            s6[h, pl.ds(i, TILE), :] = nn(tile, upd[h]).astype(BF)
-
-        tiled(RR, fn)
+            tile = root[pl.ds(i // pr, MT // pr)].reshape(MT, RB)
+            s6[h, pl.ds(i, MT), :] = nn(tile, upd[h]).astype(BF)
+
         rh = RR // 2
-        send(s6.at[h, pl.ds((1 - k) * rh, rh)], r6.at[h], snd.at[h, 7], rcv.at[h, 7], sib)
+        halves(RR, fn, lambda: send(s6.at[h, pl.ds((1 - k) * rh, rh)], r6.at[h], snd.at[h, 7], rcv.at[h, 7], sib))
         sent(r6.at[h], snd.at[h, 7])
 
     def i_(h):
@@ -481,7 +565,7 @@
         arrive(rsc.at[h, pl.ds(0, RR // 2)], rcv.at[h, 10])
 
         def fn(i):
-            s8[h, pl.ds(i, TILE), :] = nn(roott[pl.ds(i, TILE), :], rsc[h]).astype(BF)
+            s8[h, pl.ds(i, MT), :] = nn(roott[pl.ds(i, MT), :], rsc[h]).astype(BF)
 
         tiled(RB, fn)
         z_scatter(h, s8, r8, pz, 11)
@@ -498,10 +582,10 @@
         exchanged(h, r10, 13)
 
         def fn(i):
-            s11[h, pl.ds(i, TILE), :] = nn(ls[pl.ds(i, TILE), :], r10[h]).astype(BF)
-
-        tiled(CR, fn)
-        col_core_send(h, s11, r11, 14)
+            s11[h, pl.ds(i, MT), :] = nn(ls[pl.ds(i, MT), :], r10[h]).astype(BF)
+
+        halves(CR, fn, lambda: col_core_send(h, s11, r11, 14))
+        sent(r11.at[h], snd.at[h, 14])
 
     def p_(h):
         col_y_send(h, s11, r11, s11b, r11b, 14)
@@ -518,44 +602,74 @@
         col_gathered(h, res, 16)
 
         def fn(i):
-            s13[h, pl.ds(i, TILE), :] = nn(invt[pl.ds(i, TILE), :], res[h]).astype(BF)
+            s13[h, pl.ds(i, MT), :] = nn(invt[pl.ds(i, MT), :], res[h]).astype(BF)
 
         tiled(CC, fn)
-        z_scatter(h, s13, r13, pu, 18)
+        if RST:
+            z_tree_scatter(h, s13, mid, r13, pu, 18)
+        else:
+            z_scatter(h, s13, r13, pu, 18)
+
+    def s2_(h):
+        if RST:
+            z_tree_pass(h, s13, mid, r13, pu, 18)
 
     def t_(h):
-        z_gather(h, cs, z_sum(h, s13, r13, pu, 18).astype(BF), pu, 19)
+        gather = z_tree if TREE else z_gather
+        gather(h, cs, (z_tree_sum if RST else z_sum)(h, s13, r13, pu, 18).astype(BF), pu, 20)
+
+    def t2_(h):
+        if TREE:
+            z_tree_forward(h, cs, pu, 20)
 
     def u_(h):
-        z_gathered(h, cs, pu, 19)
+        arrive(cs.at[h, pl.ds(0, (Z - 3 if TREE else Z - 1) * pu)], rcv.at[h, 20])
         out_c[:, h * W : (h + 1) * W] = cs[h]
 
+    def first(h):
+        fn = a1(h)
+        if h == 0:
+            small_loads[7].wait()
+            pl.semaphore_wait(barrier, Q - 1 + Z - 1)
+        halves(CR, fn, lambda: col_core_send(h, s1, r1, 0))
+        sent(r1.at[h], snd.at[h, 0])
+
+    def coefs():
+        for n in range(6):
+            small_loads[n].wait()
+        make_coefs()
+        at = pl.ds(pl.multiple_of(k * half + y * pc, pc), pc)
+        for h in range(H):
+            scaled[h] = pivot(sol[h, at, :].astype(F32), cfa, cfb, c * pc, pc)
+
+    small_loads[6].wait()
+    make_slots()
     for n in range(3):
         loads[n].wait()
     mask_child()
-    for h in range(H):
-        a1(h)
-    pl.semaphore_wait(barrier, Q - 1 + Z - 1)
-    plan = [
-        (a2, [make_slots, make_sel]),
-        (b, [send_meta, make_coefs, make_lst]),
-        (cc, [make_ident]),
-        (d, []),
-        (e, [make_asm, mask_root]),
-        (f, [make_ls]),
-        (g, [lambda: transpose_into(root, roott, RR, RB, pr)]),
-        (hh, []),
-        (i_, [make_asmt]),
-        (j_, [lambda: transpose_into(inv, invt, CR, CC, pc)]),
-        (k_, []), (l_, []), (m_, []), (n_, []), (o_, []), (p_, []), (q_, []), (r_, []), (s_, []), (t_, []), (u_, []),
-    ]
-    for stage, background in plan:
-        if stage is g:
-            loads[7].wait()
-        for h in range(H):
-            stage(h)
-        for work in background:
-            work()
+    local = {
+        "sel": make_sel,
+        "meta": send_meta,
+        "lst0": lambda: make_lst(0),
+        "lst1": lambda: make_lst(1),
+        "ident": make_ident,
+        "asm": make_asm,
+        "coefs": coefs,
+        "mask": mask_root,
+        "roott": lambda: transpose_into(root, roott, RR, RB, pr),
+        "ls0": lambda: make_ls(0),
+        "ls1": lambda: make_ls(1),
+        "asmt": make_asmt,
+        "invt": lambda: transpose_into(inv, invt, CR, CC, pc),
+        "rrhs": loads[7].wait,
+    }
+    steps = [first, b, cc, d, e, f, g, hh, i_, j_, k_, l_, m_, n_, o_, p_, q_, r_, s_, s2_, t_, t2_, u_]
+    names = dict(zip("abcdefghijklmnopqrsStTu", steps))
+    for item in ORDER:
+        if item in local:
+            local[item]()
+        else:
+            names[item[0]](int(item[1]))
     for view, sem in pending:
         arrive(view, sem)
 
@@ -583,9 +697,10 @@
         chain((Z - 1) * pz), chain(RB),
         chain(RR), chain(RR // 2), chain(RR // 2), chain((G - 1) * pr), chain(RR), chain(RB), chain((Z - 1) * pz),
         chain(RB), chain(NS), chain(NS),
-        chain(CR), chain(half), chain(half), chain((Y - 1) * pc), chain(CR), chain(CC), chain((Z - 1) * pu), chain(CC),
-        pltpu.SemaphoreType.DMA((8,)), pltpu.SemaphoreType.DMA((H, 20)), pltpu.SemaphoreType.DMA((H, 20)),
-        pltpu.SemaphoreType.DMA((H, 2, Y - 1)), pltpu.SemaphoreType.DMA((2,)),
+        chain(CR), chain(half), chain(half), chain((Y - 1) * pc), chain(CR), chain(CC), chain((Z - 1) * pu), chain(3 * pu), chain(CC),
+        *[pltpu.VMEM((1, n), dt) for n, dt in ((CR, F32), (CR, F32), (CR, jnp.int32), (RR, F32), (RR, F32), (RR, jnp.int32), (U, jnp.int32), (1, jnp.int32))],
+        pltpu.SemaphoreType.DMA((8,)), pltpu.SemaphoreType.DMA((8,)), pltpu.SemaphoreType.DMA((H, 21)), pltpu.SemaphoreType.DMA((H, 21)),
+        pltpu.SemaphoreType.DMA((H, 2, Y - 1)), pltpu.SemaphoreType.DMA((H, 4)), pltpu.SemaphoreType.DMA((2,)),
     ]
     anyspec = pl.BlockSpec(memory_space=pl.ANY)
     vspec = pl.BlockSpec(memory_space=pltpu.VMEM)
@@ -593,8 +708,8 @@
     child, rooted = pl.pallas_call(
         functools.partial(body, dims),
         name="substitution",
-        out_shape=(jax.ShapeDtypeStruct((CC, R), BF), jax.ShapeDtypeStruct((RB, R), BF)),
-        in_specs=[anyspec] * 5 + [vspec] * 7 + [pl.BlockSpec(memory_space=pltpu.SMEM)],
+        out_shape=(OUT((CC, R), BF), OUT((RB, R), BF)),
+        in_specs=[anyspec] * 13,
         out_specs=(vspec, vspec),
         scratch_shapes=scratch,
         cost_estimate=pl.CostEstimate(flops=flops, bytes_accessed=8 << 20, transcendentals=0),
@@ -612,7 +727,7 @@
         root_off.reshape(1, RR),
         root_pattern.reshape(1, RR),
         child_map.reshape(1, U),
-        child_pivots,
+        child_pivots.reshape(1, 1),
     )
     return (child.astype(F32)[None], rooted.astype(F32))
 

time: 150 us -> 132 us (0.88); the launches traced: 148 us -> 132 us
  Pallas kernels: 143 us -> 128 us
  other arithmetic: 3.86 us -> 1.87 us
    pallas_call x1, Pallas kernels: 143 us -> 128 us  [shards(): pl.pallas_call(functools.partial(body, dims), name='substitution', out_sh...]
where the time goes in v2:
time: 132 us
  Pallas kernels  128 us (97%)
  other arithmetic  1.87 us (1%)
    pallas_call x1, Pallas kernels, shards(): pl.pallas_call(functools.partial(body, dims), name='substitution', out_sh...  128 us

profile of v2, /device:TPU:2, one launch (start us, length us, event | category | flops | bytes accessed | tf_op | source)
XLA Modules:
  0.0 131.6 jit_solution(17389386310146058875)
XLA Ops:
  1.3 128.4 %substitution.1 = (bf16[1024,256]{1,0:T(8,128)(2,1)S(1)}, bf16[512,256]{1,0:T(8,128)(2,1)S(1)}) custom-call(bf16[4,2,128,1024]{3,2,1,0:T(8,128)(2,1)} %bitcast.12, bf16[4,2,128,1024]{3,2,1,0:T(8,128)(2,1)} %bitcast.13, bf16[16,2,64,512]{3,2,1,0:T(8,128)(2,1)} %bitcast.14, bf16[1024,256]{1,0:T(8,128)(2,1)} %bitcast.15, bf16[512,256]{1,0:T(8,128)(2,1)} %refs_4_.1, ...), custom_call_target="tpu_custom_call" | custom-call | flops 5368709120 | bytes 8388608 | tf_op jit(solution)/shard_map/substitution/pallas_call | solution.py:708
  129.7 1.0 bitcast_convert_fusion
  130.8 0.8 convert_element_type.4

commit v3 on v2

--- a/solution.py
+++ b/solution.py
@@ -15,14 +15,14 @@
 TILE = 256
 MT = 512
 XT = 256
-UNROLL = False
 CHAINS = 2
-ORDER = ["a0", "a1", "sel", "b0", "b1", "meta", "lst0", "c0", "c1", "ident", "lst1", "d0", "d1", "e0", "e1"]
-ORDER += ["asm", "f0", "rrhs", "mask", "coefs", "f1", "roott", "g0", "g1", "h0", "i0", "h1", "i1", "j0", "asmt"]
+ORDER = ["sel", "b0", "b1", "meta", "lst0", "c0", "c1", "ident", "lst1", "d0", "e0", "d1"]
+ORDER += ["asm", "coefs", "mask", "e1", "roott", "f0", "rrhs", "f1", "g0", "g1", "h0", "i0", "h1", "i1", "j0", "asmt"]
 ORDER += ["j1", "k0", "l0", "k1", "l1", "ls0", "m0", "ls1", "m1", "n0", "n1", "invt", "o0", "p0", "o1", "q0", "p1"]
 ORDER += ["r0", "q1", "s0", "r1", "s1", "S0", "S1", "t0", "t1", "T0", "T1", "u0", "u1"]
 TREE = True
 RST = False
+ZH = False
 OUT = pltpu.VMEM
 
 
@@ -98,8 +98,8 @@
     small_loads[6].start()
     for ld in loads[:3]:
         ld.start()
-    lax.fori_loop(1, Q, greet_plane, 0, unroll=UNROLL)
-    lax.fori_loop(1, Z, greet_z, 0, unroll=UNROLL)
+    lax.fori_loop(1, Q, greet_plane, 0)
+    lax.fori_loop(1, Z, greet_z, 0)
     for ld in small_loads[7:] + loads[3:] + small_loads[:6]:
         ld.start()
 
@@ -320,6 +320,9 @@
         coefficients(cdiag, coff, cpat, cfa, cfb, c * pc, pc)
         coefficients(rdiag, roff, rpat, rfa, rfb, me * pr, pr)
 
+    def away(i, size):
+        return size // 2 + (1 - 2 * (i % 2)) * ((i + 1) // 2)
+
     half = CR // 2
 
     def col_core_send(h, s_a, r_a, st):
@@ -328,7 +331,7 @@
     def col_y_send(h, s_a, r_a, s_b, r_b, st):
         arrive(r_a.at[h], rcv.at[h, st])
         s_b[h] = (s_a[h, pl.ds(pl.multiple_of(k * half, half), half), :].astype(F32) + r_a[h].astype(F32)).astype(BF)
-        for d in range(1, Y):
+        for d in [away(n, Y) for n in range(Y - 1)]:
             p = (y + d) % Y
             send(s_b.at[h, pl.ds(p * pc, pc)], r_b.at[h, pl.ds((d - 1) * pc, pc)], snd.at[h, st + 1], rcv.at[h, st + 1], y_id(d))
         sent(r_b.at[h], snd.at[h, st + 1])
@@ -343,7 +346,7 @@
     def col_gather(h, buf, value, st, ys):
         at = pl.ds(pl.multiple_of(k * half + y * pc, pc), pc)
         buf[h, at, :] = value
-        for d in range(1, Y):
+        for d in [away(n, Y) for n in range(Y - 1)]:
             send(buf.at[h, at], buf.at[h, at], snd.at[h, st], ysem.at[h, ys, d - 1], y_id(d))
         send(buf.at[h, at], buf.at[h, at], snd.at[h, st + 1], rcv.at[h, st + 1], sib)
         sent(buf.at[h, pl.ds(0, (Y - 1) * pc)], snd.at[h, st])
@@ -359,7 +362,10 @@
         arrive(buf.at[h, pl.ds(0, half)], rcv.at[h, st + 1])
 
     def far(i):
-        return Z // 2 + (1 - 2 * (i % 2)) * ((i + 1) // 2)
+        return away(i, Z)
+
+    def chip(n):
+        return (t + away(n // Y, T)) % T * Y + (y + away(n % Y, Y)) % Y
 
     def z_scatter(h, s, rr, n, st):
         def step(i, carry):
@@ -368,7 +374,28 @@
             send(s.at[h, pl.ds(to * n, n)], rr.at[h, pl.ds((d - 1) * n, n)], snd.at[h, st], rcv.at[h, st], z_id(d))
             return carry
 
-        lax.fori_loop(0, Z - 1, step, 0, unroll=UNROLL)
+        lax.fori_loop(0, Z - 1, step, 0)
+        sent(rr.at[h], snd.at[h, st])
+
+    def z_product(h, mat, vec, s, rr, n, st):
+        side = Z // 2
+        rows = side * n
+
+        def step(i, carry):
+            g = (r // side + 1 + i) % 2
+            at = pl.multiple_of(g * rows, rows)
+            s[h, pl.ds(at, rows), :] = nn(mat[pl.ds(at, rows), :], vec[h]).astype(BF)
+            for j in range(side):
+                to = g * side + j
+
+                @pl.when(to != r)
+                def _():
+                    d = (to - r + Z) % Z
+                    send(s.at[h, pl.ds(to * n, n)], rr.at[h, pl.ds((d - 1) * n, n)], snd.at[h, st], rcv.at[h, st], (t, to, c))
+
+            return carry
+
+        lax.fori_loop(0, 2, step, 0)
         sent(rr.at[h], snd.at[h, st])
 
     def z_sum(h, s, rr, n, st):
@@ -386,7 +413,7 @@
             send(buf.at[h, at], buf.at[h, at], snd.at[h, st], rcv.at[h, st], z_id(far(i)))
             return carry
 
-        lax.fori_loop(0, Z - 1, step, 0, unroll=UNROLL)
+        lax.fori_loop(0, Z - 1, step, 0)
         sent(buf.at[h, pl.ds(0, (Z - 1) * n)], snd.at[h, st])
 
     def z_gathered(h, buf, n, st):
@@ -469,14 +496,6 @@
         rows = r * CR + c * pc + lax.broadcasted_iota(jnp.int32, (pc, W), 0)
         return rows < piv[...]
 
-    def a1(h):
-        def fn(i):
-            p = i // pc
-            tile = inv[pl.ds(p, MT // pc)].reshape(MT, CC)
-            s1[h, pl.ds(i, MT), :] = nn(tile, rhs[:, h * W : (h + 1) * W]).astype(BF)
-
-        return fn
-
     def b(h):
         col_y_send(h, s1, r1, s2, r2, 0)
 
@@ -494,6 +513,9 @@
 
     def f(h):
         exchanged(h, r3, 4)
+        if ZH:
+            z_product(h, asm, r3, s4, r4, pz, 5)
+            return
 
         def fn(i):
             s4[h, pl.ds(i, MT), :] = nn(asm[pl.ds(i, MT), :], r3[h]).astype(BF)
@@ -523,7 +545,7 @@
         gi = t * Y + y
 
         def step(j, carry):
-            p = (gi + 1 + j) % G
+            p = chip(j)
             at = pl.ds(pl.multiple_of(p * pr, pr), pr)
             mine = pl.ds(pl.multiple_of(k * rh + p * pr, pr), pr)
             s6b[h, at, :] = (s6[h, mine, :].astype(F32) + r6[h, at, :].astype(F32)).astype(BF)
@@ -548,7 +570,7 @@
         rsc[h, at, :] = value
 
         def step(n, carry):
-            send(rsc.at[h, at], rsc.at[h, at], snd.at[h, 9], rcv.at[h, 9], g_id((gi + n) % G))
+            send(rsc.at[h, at], rsc.at[h, at], snd.at[h, 9], rcv.at[h, 9], g_id(chip(n - 1)))
             return carry
 
         lax.fori_loop(1, G, step, 0)
@@ -563,6 +585,9 @@
 
     def l_(h):
         arrive(rsc.at[h, pl.ds(0, RR // 2)], rcv.at[h, 10])
+        if ZH:
+            z_product(h, roott, rsc, s8, r8, pz, 11)
+            return
 
         def fn(i):
             s8[h, pl.ds(i, MT), :] = nn(roott[pl.ds(i, MT), :], rsc[h]).astype(BF)
@@ -600,6 +625,9 @@
 
     def s_(h):
         col_gathered(h, res, 16)
+        if ZH:
+            z_product(h, invt, res, s13, r13, pu, 18)
+            return
 
         def fn(i):
             s13[h, pl.ds(i, MT), :] = nn(invt[pl.ds(i, MT), :], res[h]).astype(BF)
@@ -626,13 +654,14 @@
         arrive(cs.at[h, pl.ds(0, (Z - 3 if TREE else Z - 1) * pu)], rcv.at[h, 20])
         out_c[:, h * W : (h + 1) * W] = cs[h]
 
-    def first(h):
-        fn = a1(h)
-        if h == 0:
-            small_loads[7].wait()
-            pl.semaphore_wait(barrier, Q - 1 + Z - 1)
-        halves(CR, fn, lambda: col_core_send(h, s1, r1, 0))
-        sent(r1.at[h], snd.at[h, 0])
+    def first(start):
+        def fn(i):
+            at = pl.multiple_of(start + i, MT)
+            value = nn(inv[pl.ds(at // pc, MT // pc)].reshape(MT, CC), rhs[...]).astype(BF)
+            for h in range(H):
+                s1[h, pl.ds(at, MT), :] = value[:, h * W : (h + 1) * W]
+
+        tiled(half, fn)
 
     def coefs():
         for n in range(6):
@@ -647,6 +676,13 @@
     for n in range(3):
         loads[n].wait()
     mask_child()
+    first((1 - k) * half)
+    small_loads[7].wait()
+    pl.semaphore_wait(barrier, Q - 1 + Z - 1)
+    for h in range(H):
+        col_core_send(h, s1, r1, 0)
+        sent(r1.at[h], snd.at[h, 0])
+    first(k * half)
     local = {
         "sel": make_sel,
         "meta": send_meta,
@@ -663,8 +699,8 @@
         "invt": lambda: transpose_into(inv, invt, CR, CC, pc),
         "rrhs": loads[7].wait,
     }
-    steps = [first, b, cc, d, e, f, g, hh, i_, j_, k_, l_, m_, n_, o_, p_, q_, r_, s_, s2_, t_, t2_, u_]
-    names = dict(zip("abcdefghijklmnopqrsStTu", steps))
+    steps = [b, cc, d, e, f, g, hh, i_, j_, k_, l_, m_, n_, o_, p_, q_, r_, s_, s2_, t_, t2_, u_]
+    names = dict(zip("bcdefghijklmnopqrsStTu", steps))
     for item in ORDER:
         if item in local:
             local[item]()

time: 132 us -> 130 us (0.985)
  Pallas kernels: 128 us -> 126 us
    pallas_call x1, Pallas kernels: 128 us -> 126 us  [shards(): pl.pallas_call(functools.partial(body, dims), name='substitution', out_sh...]
where the time goes in v3:
time: 130 us; the launch traced here: 129 us
  Pallas kernels  126 us (97%)
  other arithmetic  1.87 us (1%)
    pallas_call x1, Pallas kernels, shards(): pl.pallas_call(functools.partial(body, dims), name='substitution', out_sh...  126 us

profile of v3, /device:TPU:2, one launch (start us, length us, event | category | flops | bytes accessed | tf_op | source)
XLA Modules:
  0.0 129.5 jit_solution(5565773187398429934)
XLA Ops:
  1.3 126.3 %substitution.1 = (bf16[1024,256]{1,0:T(8,128)(2,1)S(1)}, bf16[512,256]{1,0:T(8,128)(2,1)S(1)}) custom-call(bf16[4,2,128,1024]{3,2,1,0:T(8,128)(2,1)} %bitcast.12, bf16[4,2,128,1024]{3,2,1,0:T(8,128)(2,1)} %bitcast.13, bf16[16,2,64,512]{3,2,1,0:T(8,128)(2,1)} %bitcast.14, bf16[1024,256]{1,0:T(8,128)(2,1)} %bitcast.15, bf16[512,256]{1,0:T(8,128)(2,1)} %refs_4_.1, ...), custom_call_target="tpu_custom_call" | custom-call | flops 5368709120 | bytes 8388608 | tf_op jit(solution)/shard_map/substitution/pallas_call | solution.py:744
  127.6 1.0 bitcast_convert_fusion
  128.7 0.8 convert_element_type.4

commit v4 on v3

--- a/solution.py
+++ b/solution.py
@@ -601,7 +601,7 @@
     def n_(h):
         z_gathered(h, rs, pz, 12)
         exchange(h, asmt, rs, s10, r10, 13)
-        out_r[:, h * W : (h + 1) * W] = rs[h]
+        out_r[:, h * W : (h + 1) * W] = rs[h].astype(F32)
 
     def o_(h):
         exchanged(h, r10, 13)
@@ -652,7 +652,7 @@
 
     def u_(h):
         arrive(cs.at[h, pl.ds(0, (Z - 3 if TREE else Z - 1) * pu)], rcv.at[h, 20])
-        out_c[:, h * W : (h + 1) * W] = cs[h]
+        out_c[:, h * W : (h + 1) * W] = cs[h].astype(F32)
 
     def first(start):
         def fn(i):
@@ -744,7 +744,7 @@
     child, rooted = pl.pallas_call(
         functools.partial(body, dims),
         name="substitution",
-        out_shape=(OUT((CC, R), BF), OUT((RB, R), BF)),
+        out_shape=(OUT((CC, R), F32), OUT((RB, R), F32)),
         in_specs=[anyspec] * 13,
         out_specs=(vspec, vspec),
         scratch_shapes=scratch,
@@ -765,7 +765,7 @@
         child_map.reshape(1, U),
         child_pivots.reshape(1, 1),
     )
-    return (child.astype(F32)[None], rooted.astype(F32))
+    return (child[None], rooted)
 
 
 def solution(mesh):

time: 130 us -> 130 us (level)
  other arithmetic: 1.87 us -> 0 us
  local copies, waits for them, and re-layouts: 0 us -> 1.77 us
    unnamed x0 -> x2, local copies, waits for them, and re-layouts: none -> 1.77 us
where the time goes in v4:
time: 130 us; the launch traced here: 129 us
  Pallas kernels  126 us (97%)
  local copies, waits for them, and re-layouts  1.77 us (1%)
    pallas_call x1, Pallas kernels, shards(): pl.pallas_call(functools.partial(body, dims), name='substitution', out_sh...  126 us

profile of v4, /device:TPU:2, one launch (start us, length us, event | category | flops | bytes accessed | tf_op | source)
XLA Modules:
  0.0 129.4 jit_solution(4786696677142523239)
XLA Ops:
  1.3 126.3 %substitution.1 = (f32[1024,256]{1,0:T(8,128)S(1)}, f32[512,256]{1,0:T(8,128)S(1)}) custom-call(bf16[4,2,128,1024]{3,2,1,0:T(8,128)(2,1)} %bitcast.11, bf16[4,2,128,1024]{3,2,1,0:T(8,128)(2,1)} %bitcast.12, bf16[16,2,64,512]{3,2,1,0:T(8,128)(2,1)} %bitcast.13, bf16[1024,256]{1,0:T(8,128)(2,1)} %bitcast.14, bf16[512,256]{1,0:T(8,128)(2,1)} %refs_4_.1, ...), custom_call_target="tpu_custom_call" | custom-call | flops 5368709120 | bytes 8388608 | tf_op jit(solution)/shard_map/substitution/pallas_call | solution.py:744
  127.6 1.0 copy.17
  128.6 0.8 copy.18

commit v5 on v4

--- a/solution.py
+++ b/solution.py
@@ -583,16 +583,16 @@
         send(rsc.at[h, mine], rsc.at[h, mine], snd.at[h, 10], rcv.at[h, 10], sib)
         sent(rsc.at[h, pl.ds(0, rh)], snd.at[h, 10])
 
+    def split_product(h, mat, buf, rows, wait):
+        mine = pl.ds(pl.multiple_of(k * rows, rows), rows)
+        rest = pl.ds(pl.multiple_of((1 - k) * rows, rows), rows)
+        part = nn(mat[:, mine], buf[h, mine, :])
+        wait()
+        return (part + nn(mat[:, rest], buf[h, rest, :])).astype(BF)
+
     def l_(h):
-        arrive(rsc.at[h, pl.ds(0, RR // 2)], rcv.at[h, 10])
-        if ZH:
-            z_product(h, roott, rsc, s8, r8, pz, 11)
-            return
-
-        def fn(i):
-            s8[h, pl.ds(i, MT), :] = nn(roott[pl.ds(i, MT), :], rsc[h]).astype(BF)
-
-        tiled(RB, fn)
+        rh = RR // 2
+        s8[h] = split_product(h, roott, rsc, rh, lambda: arrive(rsc.at[h, pl.ds(0, rh)], rcv.at[h, 10]))
         z_scatter(h, s8, r8, pz, 11)
 
     def m_(h):
@@ -624,15 +624,7 @@
         col_forward(h, res, 16, 1)
 
     def s_(h):
-        col_gathered(h, res, 16)
-        if ZH:
-            z_product(h, invt, res, s13, r13, pu, 18)
-            return
-
-        def fn(i):
-            s13[h, pl.ds(i, MT), :] = nn(invt[pl.ds(i, MT), :], res[h]).astype(BF)
-
-        tiled(CC, fn)
+        s13[h] = split_product(h, invt, res, half, lambda: col_gathered(h, res, 16))
         if RST:
             z_tree_scatter(h, s13, mid, r13, pu, 18)
         else:

time: 130 us -> 130 us (level)
  no operation moved by 1% of the time
where the time goes in v5:
time: 130 us
  Pallas kernels  127 us (98%)
  local copies, waits for them, and re-layouts  1.77 us (1%)
    pallas_call x1, Pallas kernels, shards(): pl.pallas_call(functools.partial(body, dims), name='substitution', out_sh...  127 us

profile of v5, /device:TPU:2, one launch (start us, length us, event | category | flops | bytes accessed | tf_op | source)
XLA Modules:
  0.0 130.1 jit_solution(17850871578501432291)
XLA Ops:
  1.3 127.1 %substitution.1 = (f32[1024,256]{1,0:T(8,128)S(1)}, f32[512,256]{1,0:T(8,128)S(1)}) custom-call(bf16[4,2,128,1024]{3,2,1,0:T(8,128)(2,1)} %bitcast.11, bf16[4,2,128,1024]{3,2,1,0:T(8,128)(2,1)} %bitcast.12, bf16[16,2,64,512]{3,2,1,0:T(8,128)(2,1)} %bitcast.13, bf16[1024,256]{1,0:T(8,128)(2,1)} %bitcast.14, bf16[512,256]{1,0:T(8,128)(2,1)} %refs_4_.1, ...), custom_call_target="tpu_custom_call" | custom-call | flops 5368709120 | bytes 8388608 | tf_op jit(solution)/shard_map/substitution/pallas_call | solution.py:736
  128.4 1.0 copy.17
  129.3 0.8 copy.18
